TPU v7x, 128 devices: a whole 4x4x4 slice. The times are simulated.
128 devices in a mesh: seg: 16 (over y_lo, x, core), chan: 8 (over y_hi, z).
Axes of the slice: x: 4, y: 4 (y_hi: 2, y_lo: 2; y = y_hi * 2 + y_lo), z: 4, core: 2. Of those that a mesh axis runs over, the one named last changes fastest.
Arguments:
- signal: bfloat16 [256, 256, 2048], P('seg', 'chan'), may hold values from -6 to 6
- latent_factor: float32 [512, 256], replicated, may hold values from -0.375 to 0.375
Outputs:
- smoothed: float32 [512, 256, 2, 256], P(None, ('seg', 'chan'))
All inputs are finite; a program needn't handle non-finite values.
Results may differ from a plain program's by a relative error of at most 0.02.
Values may be sent and summed in bfloat16 or wider, within the bound.
A program may use at most 128 MiB of HBM per device.

v0:
```python
import math
import jax
import jax.numpy as jnp
from jax import lax
from jax.sharding import PartitionSpec as P


def dft_table(length, bins):
    times = jnp.arange(length, dtype=jnp.int32)
    freqs = jnp.arange(bins, dtype=jnp.int32)
    phase = times[:, None] * freqs[None, :] % length
    theta = 2.0 * math.pi * phase.astype(jnp.float32) / length
    window = 0.5 - 0.5 * jnp.cos(2.0 * math.pi * times.astype(jnp.float32) / length)
    weight = window / jnp.sqrt(jnp.float32(3.0 * length / 8.0))
    cos_part = weight[:, None] * jnp.cos(theta)
    sin_part = -weight[:, None] * jnp.sin(theta)
    return jnp.stack([cos_part, sin_part], axis=1).astype(jnp.bfloat16)


def cross_terms(spectra, segs):
    real_part = spectra[:, :, 0, :]
    imag_part = spectra[:, :, 1, :]
    same = jnp.einsum(
        "fsc,fsd->fcd", real_part, real_part, preferred_element_type=jnp.float32
    ) + jnp.einsum("fsc,fsd->fcd", imag_part, imag_part, preferred_element_type=jnp.float32)
    twist = jnp.einsum(
        "fsc,fsd->fcd", real_part, imag_part, preferred_element_type=jnp.float32
    ) - jnp.einsum("fsc,fsd->fcd", imag_part, real_part, preferred_element_type=jnp.float32)
    return jnp.stack([same, twist], axis=2) * (1.0 / segs)


def per_device(signal, latent_factor):
    seg_count, chan_local, length = signal.shape
    bins, rank = latent_factor.shape
    n_seg = lax.axis_size("seg")
    n_chan = lax.axis_size("chan")
    segs = seg_count * n_seg
    table = dft_table(length, bins)
    spectra = jnp.einsum("scl,lkf->fskc", signal, table, preferred_element_type=jnp.float32).astype(
        jnp.bfloat16
    )
    block_bins = bins // (n_seg * n_chan)
    banded = lax.all_to_all(spectra, "chan", split_axis=0, concat_axis=3, tiled=True)
    owned = lax.psum_scatter(
        cross_terms(banded, segs).astype(jnp.bfloat16), "seg", scatter_dimension=0, tiled=True
    ).astype(jnp.float32)
    pairs = lax.all_to_all(
        owned.astype(jnp.bfloat16), ("seg", "chan"), split_axis=1, concat_axis=0, tiled=True
    ).astype(owned.dtype)
    ordered = latent_factor.reshape(n_chan, n_seg, block_bins, rank)
    ordered = jnp.transpose(ordered, (1, 0, 2, 3)).reshape(bins, rank)
    latent = jnp.einsum("fr,fckd->rckd", ordered, pairs, precision=lax.Precision.HIGHEST)
    return jnp.einsum("fr,rckd->fckd", latent_factor, latent, precision=lax.Precision.HIGHEST)


def solution(mesh):
    in_specs = (P("seg", "chan", None), P())
    out_specs = P(None, ("seg", "chan"), None, None)
    return jax.shard_map(
        per_device, mesh=mesh, in_specs=in_specs, out_specs=out_specs, check_vma=False
    )
```

profile of v0, /device:TPU:1, one launch (start us, length us, event | category | flops | bytes accessed | tf_op | source)
XLA Modules:
  0.0 369.4 jit_solution(232264247619098032)
XLA Ops:
  6.7 17.7 %multiply_convert_fusion = (bf16[2048,1,512]{2,0,1:T(8,128)(2,1)S(1)}, bf16[2048,1,512]{2,0,1:T(8,128)(2,1)S(1)}) fusion(f32[2048]{0:T(1024)S(1)} %fusion.28, f32[2048]{0:T(1024)S(1)} %subtract_multiply_fusion), kind=kLoop, calls=%fused_computation.14 | loop fusion | flops 18874368 | bytes 4210688 | tf_op jit(solution)/shard_map/convert.1
  24.4 2.3 fusion.14
  26.7 6.5 %copy.11 = bf16[512,16,2,32]{3,1,2,0:T(8,128)(2,1)} copy(bf16[512,16,2,32]{0,3,1,2:T(8,128)(2,1)S(1)} %fusion.14) | data formatting | bytes 2097152 | tf_op jit(solution)/shard_map/convert_element_type | solution.py:39
  33.2 7.0 %reshape.137 = bf16[8,2,32768]{2,1,0:T(2,128)(2,1)S(1)} reshape(bf16[512,2,16,32]{3,2,1,0:T(8,128)(2,1)} %bitcast.71) | data formatting | bytes 2097152
  40.1 23.9 %all_to_all.36 = bf16[8,2,32768]{2,1,0:T(2,128)(2,1)S(1)} all-to-all(bf16[8,2,32768]{2,1,0:T(2,128)(2,1)S(1)} %reshape.137), channel_id=1, replica_groups=mesh['seg'=16,'chan'=8] {'chan'}, dimensions={0} | all-to-all | bytes 2097152 | tf_op jit(solution)/shard_map/all_to_all | solution.py:43
  64.0 4.5 %reshape.138 = bf16[512,2,16,32]{3,2,1,0:T(8,128)(2,1)} reshape(bf16[8,2,32768]{2,1,0:T(2,128)(2,1)S(1)} %all_to_all.36) | data formatting | bytes 2097152
  68.5 4.6 %copy.12 = bf16[8,64,16,2,32]{1,4,0,3,2:T(8,128)(2,1)S(1)} copy(bf16[8,64,16,2,32]{4,2,3,1,0:T(8,128)(2,1)} %bitcast.72) | data formatting | bytes 2097152 | tf_op jit(solution)/shard_map/all_to_all | solution.py:43
  73.1 1.2 fusion.30
  74.3 1.9 copy.25
  76.2 0.8 copy.26
  77.1 8.1 %fusion.26 = f32[64,256,256]{2,1,0:T(8,128)} fusion(bf16[64,16,1,256]{3,1,0,2:T(8,128)(2,1)S(1)} %copy.25), kind=kOutput, calls=%fused_computation.33 | convolution fusion | flops 134217728 | bytes 17301504 | tf_op jit(solution)/shard_map/fsc,fsd->fcd/dot_general | solution.py:23
  85.2 8.1 %fusion.21 = f32[64,256,256]{2,1,0:T(8,128)} fusion(bf16[64,16,1,256]{3,1,0,2:T(8,128)(2,1)S(1)} %copy.26, bf16[64,16,1,256]{3,1,0,2:T(8,128)(2,1)S(1)} %copy.25), kind=kOutput, calls=%fused_computation.28 | convolution fusion | flops 134217728 | bytes 17825792 | tf_op jit(solution)/shard_map/fsc,fsd->fcd/dot_general | solution.py:26
  93.3 8.1 %subtract_bitcast_fusion = f32[64,256,1,256]{3,1,0,2:T(8,128)S(1)} fusion(f32[64,256,256]{2,1,0:T(8,128)} %fusion.21, bf16[64,16,1,256]{3,1,0,2:T(8,128)(2,1)S(1)} %copy.26, bf16[64,16,1,256]{3,1,0,2:T(8,128)(2,1)S(1)} %copy.25), kind=kOutput, calls=%fused_computation.2 | convolution fusion | flops 138412032 | bytes 34603008 | tf_op jit(solution)/shard_map/fsc,fsd->fcd/dot_general | solution.py:28
  101.4 13.9 %add_bitcast_fusion = f32[64,256,1,256]{3,1,0,2:T(8,128)} fusion(f32[64,256,256]{2,1,0:T(8,128)} %fusion.26, bf16[64,16,1,256]{3,1,0,2:T(8,128)(2,1)S(1)} %copy.26), kind=kOutput, calls=%fused_computation.3 | convolution fusion | flops 138412032 | bytes 34078720 | tf_op jit(solution)/shard_map/fsc,fsd->fcd/dot_general | solution.py:25
  115.3 15.1 %fusion = bf16[64,256,2,256]{3,1,0,2:T(8,128)(2,1)} fusion(f32[64,256,1,256]{3,1,0,2:T(8,128)S(1)} %subtract_bitcast_fusion, f32[64,256,1,256]{3,1,0,2:T(8,128)} %add_bitcast_fusion), kind=kLoop, calls=%fused_computation.1 | loop fusion | flops 25165824 | bytes 50331648 | tf_op jit(solution)/shard_map/convert_element_type | solution.py:45
  132.3 191.7 %all-reduce.3.cloned.1.call-done = bf16[64,256,2,256]{3,1,0,2:T(8,128)(2,1)} async-done(((bf16[64,256,2,256]{3,1,0,2:T(8,128)(2,1)}), bf16[64,256,2,256]{3,1,0,2:T(8,128)(2,1)}) %all-reduce.3.cloned.1.call-update) | async-done | bytes 16777232
  324.0 1.3 constant_dynamic-slice_fusion
  325.3 1.8 copy.15
  327.1 8.4 %all-to-all-start.1 = ((bf16[4,256,2,256]{3,0,2,1:T(4,128)(2,1)}), bf16[4,256,2,256]{3,0,2,1:T(4,128)(2,1)S(1)}, u32[]{:S(2)}, u32[]{:S(2)}) async-start(bf16[4,256,2,256]{3,0,2,1:T(4,128)(2,1)} %copy.15), calls=%async_computation.1 | async-start | bytes 2097152 | tf_op jit(solution)/shard_map/all_to_all | solution.py:47
  335.9 17.3 %all-to-all-done.1 = bf16[4,256,2,256]{3,0,2,1:T(4,128)(2,1)S(1)} async-done(((bf16[4,256,2,256]{3,0,2,1:T(4,128)(2,1)}), bf16[4,256,2,256]{3,0,2,1:T(4,128)(2,1)S(1)}, u32[]{:S(2)}, u32[]{:S(2)}) %all-to-all-start.1) | async-done | bytes 1048608 | tf_op jit(solution)/shard_map/all_to_all | solution.py:47
  353.2 0.8 copy.16
  354.1 1.2 convolution_bitcast_fusion.1
  355.3 3.2 convolution_bitcast_fusion
  358.5 4.1 %copy.19 = f32[512,2,2,256]{3,2,1,0:T(2,128)} copy(f32[512,2,2,256]{0,3,2,1:T(8,128)} %convolution_bitcast_fusion) | data formatting | bytes 4194304 | tf_op jit(solution)/shard_map/fr,rckd->fckd/dot_general | solution.py:53
  (16 shorter events, 1.7 us)
Async XLA Ops:
  6.5 17.8 %copy-start = (bf16[16,32,2048]{2,1,0:T(8,128)(2,1)S(1)}, bf16[16,32,2048]{2,1,0:T(8,128)(2,1)}, u32[]{:S(2)}) copy-start(bf16[16,32,2048]{2,1,0:T(8,128)(2,1)} %param.2) | copy-start | bytes 6291460
  6.5 317.5 %all-reduce.3.cloned.1.call-start = ((), (), s32[]{:S(2)}) async-start(), calls=%async_computation.2 | async-start | bytes 33554432
  130.4 0.7 copy-start.3
  130.4 205.1 %copy-start.2 = (f32[512,256]{1,0:T(8,128)S(1)}, f32[512,256]{1,0:T(8,128)}, u32[]{:S(2)}) copy-start(f32[512,256]{1,0:T(8,128)} %param.3) | copy-start | bytes 1572868
  327.1 26.1 %all-to-all-start.1 = ((bf16[4,256,2,256]{3,0,2,1:T(4,128)(2,1)}), bf16[4,256,2,256]{3,0,2,1:T(4,128)(2,1)S(1)}, u32[]{:S(2)}, u32[]{:S(2)}) async-start(bf16[4,256,2,256]{3,0,2,1:T(4,128)(2,1)} %copy.15), calls=%async_computation.1 | async-start | bytes 2097152 | tf_op jit(solution)/shard_map/all_to_all | solution.py:47
  354.1 8.5 %copy-start.1 = (bf16[16,32,2048]{2,1,0:T(8,128)(2,1)S(1)}, bf16[16,32,2048]{2,1,0:T(8,128)(2,1)}, u32[]{:S(2)}) copy-start(bf16[16,32,2048]{2,1,0:T(8,128)(2,1)} %param.2) | copy-start | bytes 6291460
Sparse Core Ops, SparseCore 0:
  130.5 193.4 all-reduce.2
where the time goes:
time: 370 us; the launch traced here: 369 us
  waiting for transfers between devices  209 us (56%)
  matrix products  45 us (12%)
  local copies, waits for them, and re-layouts  36 us (10%)
  other arithmetic  32.9 us (9%)
  blocking collectives  23.9 us (6%)
  between operations  14.2 us (4%)
  starting transfers between devices  8.41 us (2%)
    unnamed x2, waiting for transfers between devices  192 us
    all_to_all x1, blocking collectives, per_device(): lax.all_to_all(spectra, 'chan', split_axis=0, concat_axis=3, tiled=True)  23.9 us
    another operation x1, other arithmetic  17.7 us
    all_to_all x1, waiting for transfers between devices, per_device(): lax.all_to_all(owned.astype(jnp.bfloat16), ('seg', 'chan'), split_axis=1,...  17.3 us
    unnamed x14, local copies, waits for them, and re-layouts  16.7 us
    convert_element_type x1, other arithmetic, per_device(): cross_terms(banded, segs).astype(jnp.bfloat16)  15.1 us
    dot_general x1, matrix products, cross_terms(): jnp.einsum('fsc,fsd->fcd', imag_part, imag_part, preferred_element_type=j...  13.9 us
    all_to_all x1, starting transfers between devices, per_device(): lax.all_to_all(owned.astype(jnp.bfloat16), ('seg', 'chan'), split_axis=1,...  8.4 us
  transfers between devices with their start and end apart: 2, of which 2 were waited for; matrix products, arithmetic and copies ran while one was open for 0% of the time, Pallas kernels for 0%

commit v1 on v0

--- a/solution.py
+++ b/solution.py
@@ -44,8 +44,16 @@
     owned = lax.psum_scatter(
         cross_terms(banded, segs).astype(jnp.bfloat16), "seg", scatter_dimension=0, tiled=True
     ).astype(jnp.float32)
-    pairs = lax.all_to_all(
-        owned.astype(jnp.bfloat16), ("seg", "chan"), split_axis=1, concat_axis=0, tiled=True
+    pairs = jnp.concatenate(
+        lax.all_to_all(
+            jnp.stack(
+                jnp.split(owned.astype(jnp.bfloat16), lax.axis_size(("seg", "chan")), axis=1)
+            ),
+            ("seg", "chan"),
+            0,
+            0,
+        ),
+        axis=0,
     ).astype(owned.dtype)
     ordered = latent_factor.reshape(n_chan, n_seg, block_bins, rank)
     ordered = jnp.transpose(ordered, (1, 0, 2, 3)).reshape(bins, rank)

time: 370 us -> 561 us (1.52); the launches traced: 369 us -> 554 us
  local copies, waits for them, and re-layouts: 36 us -> 224 us
    unnamed x14 -> x138, local copies, waits for them, and re-layouts: 16.7 us -> 199 us
  transfers between devices with their start and end apart: 2 -> 2, of which waited for: 2 -> 2; matrix products, arithmetic and copies ran while one was open for 0% -> 1% of each run, Pallas kernels for 0% -> 0%
where the time goes in v1:
time: 561 us; the launch traced here: 554 us
  local copies, waits for them, and re-layouts  224 us (40%)
  waiting for transfers between devices  204 us (36%)
  matrix products  47 us (8%)
  other arithmetic  32.9 us (6%)
  blocking collectives  23.9 us (4%)
  between operations  14.2 us (3%)
  starting transfers between devices  8.41 us (1%)
    unnamed x138, local copies, waits for them, and re-layouts  199 us
    unnamed x2, waiting for transfers between devices  192 us
    all_to_all x1, blocking collectives, per_device(): lax.all_to_all(spectra, 'chan', split_axis=0, concat_axis=3, tiled=True)  23.9 us
    another operation x1, other arithmetic  17.7 us
    convert_element_type x1, other arithmetic, per_device(): cross_terms(banded, segs).astype(jnp.bfloat16)  15.1 us
    dot_general x1, matrix products, cross_terms(): jnp.einsum('fsc,fsd->fcd', imag_part, imag_part, preferred_element_type=j...  13.9 us
    all_to_all x1, waiting for transfers between devices, per_device(): lax.all_to_all(jnp.stack(jnp.split(owned.astype(jnp.bfloat16), lax.axis_s...  11.9 us
  transfers between devices with their start and end apart: 2, of which 2 were waited for; matrix products, arithmetic and copies ran while one was open for 1% of the time, Pallas kernels for 0%

profile of v1, /device:TPU:1, one launch (start us, length us, event | category | flops | bytes accessed | tf_op | source)
XLA Modules:
  0.0 554.1 jit_solution(10844337949519980204)
XLA Ops:
  6.7 17.7 %multiply_convert_fusion = (bf16[2048,1,512]{2,0,1:T(8,128)(2,1)S(1)}, bf16[2048,1,512]{2,0,1:T(8,128)(2,1)S(1)}) fusion(f32[2048]{0:T(1024)S(1)} %fusion.156, f32[2048]{0:T(1024)S(1)} %subtract_multiply_fusion), kind=kLoop, calls=%fused_computation.14 | loop fusion | flops 18874368 | bytes 4210688 | tf_op jit(solution)/shard_map/convert.1
  24.4 2.3 fusion.14
  26.7 6.5 %copy.11 = bf16[512,16,2,32]{3,1,2,0:T(8,128)(2,1)} copy(bf16[512,16,2,32]{0,3,1,2:T(8,128)(2,1)S(1)} %fusion.14) | data formatting | bytes 2097152 | tf_op jit(solution)/shard_map/convert_element_type | solution.py:39
  33.2 7.0 %reshape.141 = bf16[8,2,32768]{2,1,0:T(2,128)(2,1)S(1)} reshape(bf16[512,2,16,32]{3,2,1,0:T(8,128)(2,1)} %bitcast.580) | data formatting | bytes 2097152
  40.1 23.9 %all_to_all.23 = bf16[8,2,32768]{2,1,0:T(2,128)(2,1)S(1)} all-to-all(bf16[8,2,32768]{2,1,0:T(2,128)(2,1)S(1)} %reshape.141), channel_id=1, replica_groups=mesh['seg'=16,'chan'=8] {'chan'}, dimensions={0} | all-to-all | bytes 2097152 | tf_op jit(solution)/shard_map/all_to_all | solution.py:43
  64.0 4.5 reshape.142
  68.5 4.6 copy.12
  74.3 1.9 copy.24
  77.0 8.1 %fusion.26 = f32[64,256,256]{2,1,0:T(8,128)} fusion(bf16[64,16,1,256]{3,1,0,2:T(8,128)(2,1)S(1)} %copy.24), kind=kOutput, calls=%fused_computation.33 | convolution fusion | flops 134217728 | bytes 17301504 | tf_op jit(solution)/shard_map/fsc,fsd->fcd/dot_general | solution.py:23
  85.1 8.1 %fusion.21 = f32[64,256,256]{2,1,0:T(8,128)} fusion(bf16[64,16,1,256]{3,1,0,2:T(8,128)(2,1)S(1)} %copy.25, bf16[64,16,1,256]{3,1,0,2:T(8,128)(2,1)S(1)} %copy.24), kind=kOutput, calls=%fused_computation.28 | convolution fusion | flops 134217728 | bytes 17825792 | tf_op jit(solution)/shard_map/fsc,fsd->fcd/dot_general | solution.py:26
  93.2 8.1 %subtract_bitcast_fusion = f32[64,256,1,256]{3,1,0,2:T(8,128)S(1)} fusion(f32[64,256,256]{2,1,0:T(8,128)} %fusion.21, bf16[64,16,1,256]{3,1,0,2:T(8,128)(2,1)S(1)} %copy.25, bf16[64,16,1,256]{3,1,0,2:T(8,128)(2,1)S(1)} %copy.24), kind=kOutput, calls=%fused_computation.2 | convolution fusion | flops 138412032 | bytes 34603008 | tf_op jit(solution)/shard_map/fsc,fsd->fcd/dot_general | solution.py:28
  101.4 13.9 %add_bitcast_fusion = f32[64,256,1,256]{3,1,0,2:T(8,128)} fusion(f32[64,256,256]{2,1,0:T(8,128)} %fusion.26, bf16[64,16,1,256]{3,1,0,2:T(8,128)(2,1)S(1)} %copy.25), kind=kOutput, calls=%fused_computation.3 | convolution fusion | flops 138412032 | bytes 34078720 | tf_op jit(solution)/shard_map/fsc,fsd->fcd/dot_general | solution.py:25
  115.3 15.1 %fusion = bf16[64,256,2,256]{3,1,0,2:T(8,128)(2,1)} fusion(f32[64,256,1,256]{3,1,0,2:T(8,128)S(1)} %subtract_bitcast_fusion, f32[64,256,1,256]{3,1,0,2:T(8,128)} %add_bitcast_fusion), kind=kLoop, calls=%fused_computation.1 | loop fusion | flops 25165824 | bytes 50331648 | tf_op jit(solution)/shard_map/convert_element_type | solution.py:45
  132.2 191.7 %all-reduce.3.cloned.1.call-done = bf16[64,256,2,256]{3,1,0,2:T(8,128)(2,1)} async-done(((bf16[64,256,2,256]{3,1,0,2:T(8,128)(2,1)}), bf16[64,256,2,256]{3,1,0,2:T(8,128)(2,1)}) %all-reduce.3.cloned.1.call-update) | async-done | bytes 16777232
  325.3 1.5 constant_dynamic-update-slice_fusion.126
  326.8 1.5 constant_dynamic-update-slice_fusion.125
  509.4 8.4 %all-to-all-start.1 = ((bf16[128,4,2,2,256]{4,2,1,3,0:T(2,128)(2,1)}), bf16[128,4,2,2,256]{4,2,1,3,0:T(2,128)(2,1)S(1)}, u32[]{:S(2)}, u32[]{:S(2)}) async-start(bf16[128,4,2,2,256]{4,2,1,3,0:T(2,128)(2,1)} %constant_dynamic-update-slice_fusion), calls=%async_computation.1 | async-start | bytes 2097152 | tf_op jit(solution)/shard_map/all_to_all | solution.py:48
  517.8 2.0 reshape.131
  519.8 1.9 copy.29
  521.7 2.0 reshape.135
  523.7 11.9 %all-to-all-done.1 = bf16[128,4,2,2,256]{4,2,1,3,0:T(2,128)(2,1)S(1)} async-done(((bf16[128,4,2,2,256]{4,2,1,3,0:T(2,128)(2,1)}), bf16[128,4,2,2,256]{4,2,1,3,0:T(2,128)(2,1)S(1)}, u32[]{:S(2)}, u32[]{:S(2)}) %all-to-all-start.1) | async-done | bytes 1048608 | tf_op jit(solution)/shard_map/all_to_all | solution.py:48
  536.6 2.2 convolution_bitcast_fusion.1
  538.9 4.2 convolution_bitcast_fusion
  543.1 4.1 copy.18
  (140 shorter events, 186.9 us)
Async XLA Ops:
  6.5 17.8 %copy-start = (bf16[16,32,2048]{2,1,0:T(8,128)(2,1)S(1)}, bf16[16,32,2048]{2,1,0:T(8,128)(2,1)}, u32[]{:S(2)}) copy-start(bf16[16,32,2048]{2,1,0:T(8,128)(2,1)} %param.2) | copy-start | bytes 6291460
  6.5 317.4 %all-reduce.3.cloned.1.call-start = ((), (), s32[]{:S(2)}) async-start(), calls=%async_computation.2 | async-start | bytes 33554432
  130.3 0.7 copy-start.2
  130.3 416.9 %copy-start.1 = (bf16[16,32,2048]{2,1,0:T(8,128)(2,1)S(1)}, bf16[16,32,2048]{2,1,0:T(8,128)(2,1)}, u32[]{:S(2)}) copy-start(bf16[16,32,2048]{2,1,0:T(8,128)(2,1)} %param.2) | copy-start | bytes 6291460
  509.4 26.1 %all-to-all-start.1 = ((bf16[128,4,2,2,256]{4,2,1,3,0:T(2,128)(2,1)}), bf16[128,4,2,2,256]{4,2,1,3,0:T(2,128)(2,1)S(1)}, u32[]{:S(2)}, u32[]{:S(2)}) async-start(bf16[128,4,2,2,256]{4,2,1,3,0:T(2,128)(2,1)} %constant_dynamic-update-slice_fusion), calls=%async_computation.1 | async-start | bytes 2097152 | tf_op jit(solution)/shard_map/all_to_all | solution.py:48
Sparse Core Ops, SparseCore 0:
  130.5 193.4 all-reduce.2
